TPU v7x, 256 devices: a whole 4x4x8 slice. The times are simulated.
256 devices in a mesh: dp: 256 (over x, y, z, core).
Axes of the slice: x: 4, y: 4, z: 8, core: 2. Of those that a mesh axis runs over, the one named last changes fastest.
Arguments:
- queries: bfloat16 [65536, 3584], P('dp'), may hold values from -2 to 2, as said below
- documents: bfloat16 [65536, 3584], P('dp'), may hold values from -2 to 2, as said below
Outputs:
- log_norm: float32 [65536], P('dp')
- query_grad: float32 [65536, 3584], P('dp')
- document_grad: float32 [65536, 3584], P('dp')
Inputs may be any that keep to these rules, and one draw needn't show every extreme that they name: Real-valued embeddings; row i of documents is the positive of row i of queries. `documents`: Real-valued embeddings.
All inputs are finite; a program needn't handle non-finite values.
Results may differ from a plain program's by a relative error of at most 0.0025.
Values may be sent and summed in bfloat16 or wider, within the bound.
A program may use at most 128 MiB of HBM per device.

v0:
```python
import functools

import jax
import jax.numpy as jnp
from jax import lax
from jax.sharding import PartitionSpec as P

scale_factor = 100.0


def passed_along(value, axis, steps):
    count = lax.axis_size(axis)
    pairs = [(source, (source + steps) % count) for source in range(count)]
    return lax.ppermute(value, axis, pairs)


def scores(left_side, right_side):
    return scale_factor * lax.dot_general(
        left_side, right_side, (((1,), (1,)), ((), ())), preferred_element_type=jnp.float32
    )


def matmul(weights, values):
    return jnp.dot(weights, values, preferred_element_type=jnp.float32)


def transposed_product(weights, values):
    return lax.dot_general(
        weights, values, (((0,), (0,)), ((), ())), preferred_element_type=jnp.float32
    )


def reduce_stats(pieces):
    highest = functools.reduce(jnp.maximum, [piece.max(axis=along) for piece, along in pieces])
    summed = sum(
        (
            jnp.exp(piece - jnp.expand_dims(highest, along)).sum(axis=along)
            for piece, along in pieces
        )
    )
    return (highest, summed)


def merge_stats(first, second):
    highest = jnp.maximum(first[0], second[0])
    return (
        highest,
        first[1] * jnp.exp(first[0] - highest) + second[1] * jnp.exp(second[0] - highest),
    )


def pair_tiles(own_q, own_d, far_q, far_d):
    return (scores(own_q, far_d), scores(far_q, own_d), scores(own_q, far_q), scores(own_d, far_d))


def pair_weights(tiles, own_norm, far_norm):
    qd_near, qd_back, qq_pair, dd_pair = tiles
    own_rows = own_norm[:, None]
    own_cols = own_norm[None, :]
    far_rows = far_norm[:, None]
    far_cols = far_norm[None, :]
    w_near = (jnp.exp(qd_near - own_rows) + jnp.exp(qd_near - far_cols)).astype(jnp.bfloat16)
    w_back = (jnp.exp(qd_back - far_rows) + jnp.exp(qd_back - own_cols)).astype(jnp.bfloat16)
    w_query = (jnp.exp(qq_pair - own_rows) + jnp.exp(qq_pair - far_cols)).astype(jnp.bfloat16)
    w_document = (jnp.exp(dd_pair - own_rows) + jnp.exp(dd_pair - far_cols)).astype(jnp.bfloat16)
    return (w_near, w_back, w_query, w_document)


def own_side(weights, far_q, far_d):
    w_near, w_back, w_query, w_document = weights
    grad_q = matmul(w_near, far_d) + matmul(w_query, far_q)
    grad_d = transposed_product(w_back, far_q) + matmul(w_document, far_d)
    return (grad_q, grad_d)


def far_side(weights, own_q, own_d):
    w_near, w_back, w_query, w_document = weights
    grad_q = matmul(w_back, own_d) + transposed_product(w_query, own_q)
    grad_d = transposed_product(w_near, own_q) + transposed_product(w_document, own_d)
    return (grad_q, grad_d)


def on_device(queries, documents):
    row_count = queries.shape[0]
    diag_mask = jnp.eye(row_count, dtype=bool)
    minus_inf = jnp.float32(-jnp.inf)
    zero_value = jnp.float32(0.0)
    own_qd = scores(queries, documents)
    own_qq = scores(queries, queries)
    own_dd = scores(documents, documents)
    stats = reduce_stats(
        [
            (own_qd, 1),
            (jnp.where(diag_mask, minus_inf, own_qd), 0),
            (jnp.where(diag_mask, minus_inf, own_qq), 1),
            (jnp.where(diag_mask, minus_inf, own_dd), 1),
        ]
    )
    partners = []
    current = (queries, documents)
    for offset in range(2):
        current = passed_along((current[0], current[1]), "dp", -1)
        partners.append(current)
    tile_sets = []
    for offset in range(2):
        far_q, far_d = partners[offset]
        tiles = pair_tiles(queries, documents, far_q, far_d)
        tile_sets.append(tiles)
        qd_near, qd_back, qq_pair, dd_pair = tiles
        stats = merge_stats(
            stats, reduce_stats([(qd_near, 1), (qd_back, 0), (qq_pair, 1), (dd_pair, 1)])
        )
        theirs = reduce_stats([(qd_near, 0), (qd_back, 1), (qq_pair, 0), (dd_pair, 0)])
        returned = passed_along((theirs[0], theirs[1]), "dp", offset + 1)
        stats = merge_stats(stats, returned)
    log_norm = stats[0] + jnp.log(stats[1])
    far_norms = []
    norm_now = log_norm
    for offset in range(2):
        norm_now = passed_along(norm_now, "dp", -1)
        far_norms.append(norm_now)
    row_norm = log_norm[:, None]
    col_norm = log_norm[None, :]
    diagonal = diag_mask.astype(jnp.float32)
    weight_qd = (
        jnp.exp(own_qd - row_norm)
        + jnp.where(diag_mask, zero_value, jnp.exp(own_qd - col_norm))
        - diagonal
    ).astype(jnp.bfloat16)
    weight_qq = jnp.where(
        diag_mask, zero_value, jnp.exp(own_qq - row_norm) + jnp.exp(own_qq - col_norm)
    ).astype(jnp.bfloat16)
    weight_dd = jnp.where(
        diag_mask, zero_value, jnp.exp(own_dd - row_norm) + jnp.exp(own_dd - col_norm)
    ).astype(jnp.bfloat16)
    grad_q = matmul(weight_qd, documents) + matmul(weight_qq, queries)
    grad_d = transposed_product(weight_qd, queries) + matmul(weight_dd, documents)
    for offset in range(2):
        far_q, far_d = partners[offset]
        weights = pair_weights(tile_sets[offset], log_norm, far_norms[offset])
        near_q_part, near_d_part = own_side(weights, far_q, far_d)
        grad_q = grad_q + near_q_part
        grad_d = grad_d + near_d_part
        back_q, back_d = far_side(weights, queries, documents)
        came_q, came_d = passed_along((back_q, back_d), "dp", offset + 1)
        grad_q = grad_q + came_q
        grad_d = grad_d + came_d
    return (log_norm, scale_factor * grad_q, scale_factor * grad_d)


def solution(mesh):
    return jax.shard_map(
        on_device,
        mesh=mesh,
        in_specs=(P("dp", None), P("dp", None)),
        out_specs=(P("dp"), P("dp", None), P("dp", None)),
        check_vma=False,
    )
```

profile of v0, /device:TPU:1, one launch (start us, length us, event | category | flops | bytes accessed | tf_op | source)
XLA Modules:
  0.0 356.6 jit_solution(14386325193807205257)
XLA Ops:
  0.6 3.3 collective-permute-start.1
  4.0 8.2 %collective-permute-start = (bf16[256,3584]{1,0:T(8,128)(2,1)}, bf16[256,3584]{1,0:T(8,128)(2,1)S(1)}, u32[]{:S(2)}, u32[]{:S(2)}) collective-permute-start(bf16[256,3584]{1,0:T(8,128)(2,1)} %param.3), channel_id=1, source_target_pairs={{0,255},{1,0},{2,1},{3,2},{4,3},{5,4},{6,5},{7,6},{8,7},{9,8},{10,... | collective-permute-start | bytes 5505032 | tf_op jit(solution)/shard_map/ppermute | solution.py:14
  12.2 2.8 fusion.13
  17.2 7.6 %collective-permute-done.1 = bf16[256,3584]{1,0:T(8,128)(2,1)S(1)} collective-permute-done((bf16[256,3584]{1,0:T(8,128)(2,1)}, bf16[256,3584]{1,0:T(8,128)(2,1)S(1)}, u32[]{:S(2)}, u32[]{:S(2)}) %collective-permute-start.1) | collective-permute-done | bytes 1835040 | tf_op jit(solution)/shard_map/ppermute | solution.py:14
  24.9 8.4 %collective-permute-start.4 = (bf16[256,3584]{1,0:T(8,128)(2,1)S(1)}, bf16[256,3584]{1,0:T(8,128)(2,1)S(1)}, u32[]{:S(2)}, u32[]{:S(2)}) collective-permute-start(bf16[256,3584]{1,0:T(8,128)(2,1)S(1)} %collective-permute-done.1), channel_id=1, source_target_pairs={{0,255},{1,0},{2,1},{3,2},{4,3},{5,4},{6,5},{7,6},{8,7},{9,8},{10,... | collective-permute-start | bytes 5505032 | tf_op jit(solution)/shard_map/ppermute | solution.py:14
  34.0 10.6 %collective-permute-done = bf16[256,3584]{1,0:T(8,128)(2,1)S(1)} collective-permute-done((bf16[256,3584]{1,0:T(8,128)(2,1)}, bf16[256,3584]{1,0:T(8,128)(2,1)S(1)}, u32[]{:S(2)}, u32[]{:S(2)}) %collective-permute-start) | collective-permute-done | bytes 1835040 | tf_op jit(solution)/shard_map/ppermute | solution.py:14
  44.5 8.4 %collective-permute-start.3 = (bf16[256,3584]{1,0:T(8,128)(2,1)S(1)}, bf16[256,3584]{1,0:T(8,128)(2,1)S(1)}, u32[]{:S(2)}, u32[]{:S(2)}) collective-permute-start(bf16[256,3584]{1,0:T(8,128)(2,1)S(1)} %collective-permute-done), channel_id=1, source_target_pairs={{0,255},{1,0},{2,1},{3,2},{4,3},{5,4},{6,5},{7,6},{8,7},{9,8},{10,... | collective-permute-start | bytes 5505032 | tf_op jit(solution)/shard_map/ppermute | solution.py:14
  55.9 8.3 %collective-permute-done.4 = bf16[256,3584]{1,0:T(8,128)(2,1)S(1)} collective-permute-done((bf16[256,3584]{1,0:T(8,128)(2,1)S(1)}, bf16[256,3584]{1,0:T(8,128)(2,1)S(1)}, u32[]{:S(2)}, u32[]{:S(2)}) %collective-permute-start.4) | collective-permute-done | bytes 1835040 | tf_op jit(solution)/shard_map/ppermute | solution.py:14
  65.7 18.1 %collective-permute-done.3 = bf16[256,3584]{1,0:T(8,128)(2,1)S(1)} collective-permute-done((bf16[256,3584]{1,0:T(8,128)(2,1)S(1)}, bf16[256,3584]{1,0:T(8,128)(2,1)S(1)}, u32[]{:S(2)}, u32[]{:S(2)}) %collective-permute-start.3) | collective-permute-done | bytes 1835040 | tf_op jit(solution)/shard_map/ppermute | solution.py:14
  85.4 1.7 collective-permute-start.5
  87.6 1.7 collective-permute-start.7
  89.7 12.6 %collective-permute-done.7 = f32[256]{0:T(256)S(1)} collective-permute-done((f32[256]{0:T(256)S(1)}, f32[256]{0:T(256)S(1)}, u32[]{:S(2)}, u32[]{:S(2)}) %collective-permute-start.7) | collective-permute-done | bytes 1056 | tf_op jit(solution)/shard_map/ppermute | solution.py:14
  106.5 2.7 convolution_add_fusion.2
  110.7 2.6 convolution_add_fusion.7
  115.8 2.6 convolution_add_fusion
  119.1 2.6 convolution_add_fusion.5
  125.1 50.2 %collective-permute-done.12 = f32[256,3584]{1,0:T(8,128)} collective-permute-done((f32[256,3584]{1,0:T(8,128)}, f32[256,3584]{1,0:T(8,128)}, u32[]{:S(2)}, u32[]{:S(2)}) %collective-permute-start.12) | collective-permute-done | bytes 3670048 | tf_op jit(solution)/shard_map/ppermute | solution.py:14
  175.3 2.9 fusion.4
  178.2 75.8 %collective-permute-done.9 = f32[256,3584]{1,0:T(8,128)} collective-permute-done((f32[256,3584]{1,0:T(8,128)}, f32[256,3584]{1,0:T(8,128)}, u32[]{:S(2)}, u32[]{:S(2)}) %collective-permute-start.9) | collective-permute-done | bytes 3670048 | tf_op jit(solution)/shard_map/ppermute | solution.py:14
  254.0 2.9 fusion.9
  256.9 57.8 %collective-permute-done.13 = f32[256,3584]{1,0:T(8,128)} collective-permute-done((f32[256,3584]{1,0:T(8,128)}, f32[256,3584]{1,0:T(8,128)}, u32[]{:S(2)}, u32[]{:S(2)}) %collective-permute-start.13) | collective-permute-done | bytes 3670048 | tf_op jit(solution)/shard_map/ppermute | solution.py:14
  314.7 4.7 %fusion.2 = f32[256,3584]{1,0:T(8,128)} fusion(f32[256,3584]{1,0:T(8,128)} %collective-permute-done.13, f32[256,3584]{1,0:T(8,128)S(1)} %fusion.4, f32[256,3584]{1,0:T(8,128)S(1)} %fusion.39, bf16[256,3584]{1,0:T(8,128)(2,1)S(1)} %collective-permute-done.4, f32[256,256]{1,0:T(8,128)S(1)} %get-tuple-element.56, f32[256]{0:T(256)S(1)} %collective-permute-done.10, ...), kind=kOutput, calls=%fused_computation.4 | convolution fusion | flops 473694208 | bytes 16779264 | tf_op jit(solution)/shard_map/dot_general | solution.py:28
  319.4 34.5 %collective-permute-done.11 = f32[256,3584]{1,0:T(8,128)S(1)} collective-permute-done((f32[256,3584]{1,0:T(8,128)}, f32[256,3584]{1,0:T(8,128)S(1)}, u32[]{:S(2)}, u32[]{:S(2)}) %collective-permute-start.11) | collective-permute-done | bytes 3670048 | tf_op jit(solution)/shard_map/ppermute | solution.py:14
  353.9 2.8 fusion.7
  (52 shorter events, 22.2 us)
Async XLA Ops:
  0.6 14.3 %copy-start = (bf16[256,3584]{1,0:T(8,128)(2,1)S(1)}, bf16[256,3584]{1,0:T(8,128)(2,1)}, u32[]{:S(2)}) copy-start(bf16[256,3584]{1,0:T(8,128)(2,1)} %param.3) | copy-start | bytes 5505028
  0.6 24.2 %collective-permute-start.1 = (bf16[256,3584]{1,0:T(8,128)(2,1)}, bf16[256,3584]{1,0:T(8,128)(2,1)S(1)}, u32[]{:S(2)}, u32[]{:S(2)}) collective-permute-start(bf16[256,3584]{1,0:T(8,128)(2,1)} %param.2), channel_id=1, source_target_pairs={{0,255},{1,0},{2,1},{3,2},{4,3},{5,4},{6,5},{7,6},{8,7},{9,8},{10,... | collective-permute-start | bytes 5505032 | tf_op jit(solution)/shard_map/ppermute | solution.py:14
  4.0 40.6 %collective-permute-start = (bf16[256,3584]{1,0:T(8,128)(2,1)}, bf16[256,3584]{1,0:T(8,128)(2,1)S(1)}, u32[]{:S(2)}, u32[]{:S(2)}) collective-permute-start(bf16[256,3584]{1,0:T(8,128)(2,1)} %param.3), channel_id=1, source_target_pairs={{0,255},{1,0},{2,1},{3,2},{4,3},{5,4},{6,5},{7,6},{8,7},{9,8},{10,... | collective-permute-start | bytes 5505032 | tf_op jit(solution)/shard_map/ppermute | solution.py:14
  15.0 1.5 copy-start.1
  24.9 39.3 %collective-permute-start.4 = (bf16[256,3584]{1,0:T(8,128)(2,1)S(1)}, bf16[256,3584]{1,0:T(8,128)(2,1)S(1)}, u32[]{:S(2)}, u32[]{:S(2)}) collective-permute-start(bf16[256,3584]{1,0:T(8,128)(2,1)S(1)} %collective-permute-done.1), channel_id=1, source_target_pairs={{0,255},{1,0},{2,1},{3,2},{4,3},{5,4},{6,5},{7,6},{8,7},{9,8},{10,... | collective-permute-start | bytes 5505032 | tf_op jit(solution)/shard_map/ppermute | solution.py:14
  44.5 39.3 %collective-permute-start.3 = (bf16[256,3584]{1,0:T(8,128)(2,1)S(1)}, bf16[256,3584]{1,0:T(8,128)(2,1)S(1)}, u32[]{:S(2)}, u32[]{:S(2)}) collective-permute-start(bf16[256,3584]{1,0:T(8,128)(2,1)S(1)} %collective-permute-done), channel_id=1, source_target_pairs={{0,255},{1,0},{2,1},{3,2},{4,3},{5,4},{6,5},{7,6},{8,7},{9,8},{10,... | collective-permute-start | bytes 5505032 | tf_op jit(solution)/shard_map/ppermute | solution.py:14
  55.2 34.5 %collective-permute-start.2 = (f32[256]{0:T(256)S(1)}, f32[256]{0:T(256)S(1)}, u32[]{:S(2)}, u32[]{:S(2)}) collective-permute-start(f32[256]{0:T(256)S(1)} %maximum_maximum_fusion.2), channel_id=1, source_target_pairs={{0,1},{1,2},{2,3},{3,4},{4,5},{5,6},{6,7},{7,8},{8,9},{9,10},{10,1... | collective-permute-start | bytes 3080 | tf_op jit(solution)/shard_map/ppermute | solution.py:14
  55.8 33.9 %collective-permute-start.6 = (f32[256]{0:T(256)S(1)}, f32[256]{0:T(256)S(1)}, u32[]{:S(2)}, u32[]{:S(2)}) collective-permute-start(f32[256]{0:T(256)S(1)} %add_add_fusion.1), channel_id=1, source_target_pairs={{0,1},{1,2},{2,3},{3,4},{4,5},{5,6},{6,7},{7,8},{8,9},{9,10},{10,1... | collective-permute-start | bytes 3080 | tf_op jit(solution)/shard_map/ppermute | solution.py:14
  85.4 16.9 %collective-permute-start.5 = (f32[256]{0:T(256)S(1)}, f32[256]{0:T(256)S(1)}, u32[]{:S(2)}, u32[]{:S(2)}) collective-permute-start(f32[256]{0:T(256)S(1)} %maximum_maximum_fusion), channel_id=1, source_target_pairs={{0,2},{1,3},{2,4},{3,5},{4,6},{5,7},{6,8},{7,9},{8,10},{9,11},{10,... | collective-permute-start | bytes 3080 | tf_op jit(solution)/shard_map/ppermute | solution.py:14
  87.6 14.7 %collective-permute-start.7 = (f32[256]{0:T(256)S(1)}, f32[256]{0:T(256)S(1)}, u32[]{:S(2)}, u32[]{:S(2)}) collective-permute-start(f32[256]{0:T(256)S(1)} %add_add_fusion), channel_id=1, source_target_pairs={{0,2},{1,3},{2,4},{3,5},{4,6},{5,7},{6,8},{7,9},{8,10},{9,11},{10,... | collective-permute-start | bytes 3080 | tf_op jit(solution)/shard_map/ppermute | solution.py:14
  102.3 251.6 %copy-start.2 = (f32[256]{0:T(256)}, f32[256]{0:T(256)S(1)}, u32[]{:S(2)}) copy-start(f32[256]{0:T(256)S(1)} %log_add_fusion) | copy-start | bytes 3076
  102.3 3.4 collective-permute-start.8
  109.2 66.1 %collective-permute-start.12 = (f32[256,3584]{1,0:T(8,128)}, f32[256,3584]{1,0:T(8,128)}, u32[]{:S(2)}, u32[]{:S(2)}) collective-permute-start(f32[256,3584]{1,0:T(8,128)} %convolution_add_fusion.2), channel_id=1, source_target_pairs={{0,1},{1,2},{2,3},{3,4},{4,5},{5,6},{6,7},{7,8},{8,9},{9,10},{10,1... | collective-permute-start | bytes 11010056 | tf_op jit(solution)/shard_map/ppermute | solution.py:14
  110.0 5.0 %collective-permute-start.10 = (f32[256]{0:T(256)S(1)}, f32[256]{0:T(256)S(1)}, u32[]{:S(2)}, u32[]{:S(2)}) collective-permute-start(f32[256]{0:T(256)S(1)} %collective-permute-done.8), channel_id=1, source_target_pairs={{0,255},{1,0},{2,1},{3,2},{4,3},{5,4},{6,5},{7,6},{8,7},{9,8},{10,... | collective-permute-start | bytes 3080 | tf_op jit(solution)/shard_map/ppermute | solution.py:14
  113.3 140.7 %collective-permute-start.9 = (f32[256,3584]{1,0:T(8,128)}, f32[256,3584]{1,0:T(8,128)}, u32[]{:S(2)}, u32[]{:S(2)}) collective-permute-start(f32[256,3584]{1,0:T(8,128)} %convolution_add_fusion.7), channel_id=1, source_target_pairs={{0,1},{1,2},{2,3},{3,4},{4,5},{5,6},{6,7},{7,8},{8,9},{9,10},{10,1... | collective-permute-start | bytes 11010056 | tf_op jit(solution)/shard_map/ppermute | solution.py:14
  118.4 196.3 %collective-permute-start.13 = (f32[256,3584]{1,0:T(8,128)}, f32[256,3584]{1,0:T(8,128)}, u32[]{:S(2)}, u32[]{:S(2)}) collective-permute-start(f32[256,3584]{1,0:T(8,128)} %convolution_add_fusion), channel_id=1, source_target_pairs={{0,2},{1,3},{2,4},{3,5},{4,6},{5,7},{6,8},{7,9},{8,10},{9,11},{10,... | collective-permute-start | bytes 11010056 | tf_op jit(solution)/shard_map/ppermute | solution.py:14
  121.7 232.2 %collective-permute-start.11 = (f32[256,3584]{1,0:T(8,128)}, f32[256,3584]{1,0:T(8,128)S(1)}, u32[]{:S(2)}, u32[]{:S(2)}) collective-permute-start(f32[256,3584]{1,0:T(8,128)} %convolution_add_fusion.5), channel_id=1, source_target_pairs={{0,2},{1,3},{2,4},{3,5},{4,6},{5,7},{6,8},{7,9},{8,10},{9,11},{10,... | collective-permute-start | bytes 11010056 | tf_op jit(solution)/shard_map/ppermute | solution.py:14
where the time goes:
time: 357 us
  waiting for transfers between devices  275 us (77%)
  matrix products  42.6 us (12%)
  starting transfers between devices  35.6 us (10%)
    ppermute x14, waiting for transfers between devices, passed_along(): return lax.ppermute(value, axis, pairs)  275 us
    ppermute x14, starting transfers between devices, passed_along(): return lax.ppermute(value, axis, pairs)  35.6 us
    dot_general x9, matrix products, transposed_product(): lax.dot_general(weights, values, (((0,), (0,)), ((), ())), preferred_elem...  20.3 us
    dot_general x11, matrix products, matmul(): return jnp.dot(weights, values, preferred_element_type=jnp.float32)  11.9 us
    dot_general x11, matrix products, scores(): lax.dot_general(left_side, right_side, (((1,), (1,)), ((), ())), preferre...  10.3 us
  transfers between devices with their start and end apart: 14, of which 9 were waited for; matrix products, arithmetic and copies ran while one was open for 11% of the time, Pallas kernels for 0%

commit v1 on v0

v1 whole, which is shorter than its diff:
```python
import functools

import jax
import jax.numpy as jnp
from jax import lax
from jax.experimental import pallas as pl
from jax.experimental.pallas import tpu as pltpu
from jax.sharding import PartitionSpec as P

MESH = pl.DeviceIdType.MESH
SCALE = 100.0
WIDTH = 512
STRIP = 64


def lse(*terms):
    highest = functools.reduce(jnp.maximum, terms)
    return highest + jnp.log(sum(jnp.exp(term - highest) for term in terms))


def as_column(row):
    return jnp.broadcast_to(row, (128, row.shape[1])).T[:, :1]


def as_row(column):
    return jnp.broadcast_to(column, (column.shape[0], 128)).T[:1, :]


def cross(left, right):
    return lax.dot_general(left, right, (((1,), (1,)), ((), ())), preferred_element_type=jnp.float32)


def kernel(
    count,
    q_ref,
    d_ref,
    norm_ref,
    lq_ref,
    ld_ref,
    came_ref,
    x,
    s,
    w,
    wt,
    going,
    stat,
    out_msg,
    in_msg,
    own_sem,
    near_send,
    near_recv,
    far_send,
    far_recv,
    pass_send,
    pass_recv,
    grad_send,
    grad_recv,
    msg_send,
    msg_recv,
):
    rows, depth = q_ref.shape
    both = 2 * rows
    chunks = depth // WIDTH
    strips = both // STRIP
    me = lax.axis_index("dp")
    sign = 1 - 2 * lax.rem(me, 2)
    p = me + sign
    r = lax.rem(me - sign + count, count)
    f = lax.rem(me + 2 * sign + count, count)
    g = lax.rem(me - 2 * sign + count, count)

    def remote(src, dst, send, recv, to):
        return pltpu.make_async_remote_copy(
            src_ref=src, dst_ref=dst, send_sem=send, recv_sem=recv, device_id=(to,), device_id_type=MESH
        )

    def columns(k):
        return pl.ds(pl.multiple_of(k * WIDTH, WIDTH), WIDTH)

    def own_copy(half, k):
        ref = (q_ref, d_ref)[half]
        return pltpu.make_async_copy(
            ref.at[:, columns(k)], x.at[pl.ds(half * rows, rows), columns(k)], own_sem.at[half, k]
        )

    def near_copy(half, k):
        ref = (q_ref, d_ref)[half]
        return remote(
            ref.at[:, columns(k)],
            x.at[pl.ds(both + half * rows, rows), columns(k)],
            near_send.at[half, k],
            near_recv.at[half, k],
            p,
        )

    def far_copy(half, k):
        ref = (q_ref, d_ref)[half]
        return remote(
            ref.at[:, columns(k)],
            x.at[pl.ds(2 * both + half * rows, rows), columns(k)],
            far_send.at[half, k],
            far_recv.at[half, k],
            r,
        )

    def pass_copy(k):
        return remote(
            x.at[pl.ds(2 * both, both), columns(k)],
            x.at[pl.ds(3 * both, both), columns(k)],
            pass_send.at[k],
            pass_recv.at[k],
            p,
        )

    def grad_copy(k):
        return remote(
            going.at[:, columns(k)], came_ref.at[:, columns(k)], grad_send.at[k], grad_recv.at[k], f
        )

    def message(which, to):
        return remote(out_msg.at[which], in_msg.at[which], msg_send.at[which], msg_recv.at[which], to)

    def add_scores(block, k):
        at = pl.ds(block * both, both)
        s[at, :] += cross(x[at, columns(k)], x[0:both, columns(k)])

    def strip(block, c):
        return SCALE * s[pl.ds(pl.multiple_of(block * both + c * STRIP, STRIP), STRIP), :]

    def own_index(c):
        row = lax.broadcasted_iota(jnp.int32, (STRIP, both), 0) + c * STRIP
        col = lax.broadcasted_iota(jnp.int32, (STRIP, both), 1)
        return row, col

    def column_lse(block, mask=None):
        def values(c):
            tile = strip(block, c)
            if mask is not None:
                tile = jnp.where(mask(c), -jnp.inf, tile)
            return tile

        def highest(c, so_far):
            return jnp.maximum(so_far, jnp.max(values(c), axis=0, keepdims=True))

        top = lax.fori_loop(0, strips, highest, jnp.full((1, both), -jnp.inf, jnp.float32))

        def total(c, so_far):
            return so_far + jnp.sum(jnp.exp(values(c) - top), axis=0, keepdims=True)

        return top + jnp.log(lax.fori_loop(0, strips, total, jnp.zeros((1, both), jnp.float32)))

    def row_lse(block):
        def body(c, _):
            tile = strip(block, c)
            top = jnp.max(tile, axis=1, keepdims=True)
            value = top + jnp.log(jnp.sum(jnp.exp(tile - top), axis=1, keepdims=True))
            stat[pl.ds(pl.multiple_of(c * STRIP, STRIP), STRIP), :] = jnp.broadcast_to(value, (STRIP, 128))
            return 0

        lax.fori_loop(0, strips, body, 0)
        return lse(stat[0:rows, :1], stat[rows:both, :1])

    def merged(row):
        return lse(row[:, :rows], row[:, rows:])

    def post(which, row, to):
        out_msg[which] = jnp.broadcast_to(row, (8, rows))
        message(which, to).start()

    def weigh(block, column, row):
        stat[...] = jnp.broadcast_to(jnp.concatenate([column, column], axis=0), (both, 128))

        def body(c, _):
            tile = strip(block, c)
            theirs = stat[pl.ds(pl.multiple_of(c * STRIP, STRIP), STRIP), :1]
            value = jnp.exp(tile - theirs) + jnp.exp(tile - row)
            at = pl.multiple_of(block * both + c * STRIP, STRIP)
            w[pl.ds(at, STRIP), :] = value.astype(jnp.bfloat16)
            return 0

        lax.fori_loop(0, strips, body, 0)

    def turn(block):
        at = pl.ds(block * both, both)
        wt[:, at] = w[at, :].T

    def loop(body, low=0, high=chunks):
        def step(k, _):
            body(k)
            return 0

        lax.fori_loop(low, high, step, 0)

    s[...] = jnp.zeros_like(s)
    barrier = pltpu.get_barrier_semaphore()
    for device in (p, r, f, g):
        pl.semaphore_signal(barrier, inc=1, device_id=(device,), device_id_type=MESH)
    pl.semaphore_wait(barrier, 4)

    def send(k):
        for half in range(2):
            far_copy(half, k).start()
        for half in range(2):
            own_copy(half, k).start()
            near_copy(half, k).start()

    loop(send)

    def on_chip(k):
        for half in range(2):
            own_copy(half, k).wait()
            near_copy(half, k).wait_recv()
        add_scores(0, k)
        add_scores(1, k)

    loop(on_chip)

    def masked(c):
        row, col = own_index(c)
        same = lax.rem(row, rows) == lax.rem(col, rows)
        return same & ~((row >= rows) & (col < rows))

    chip_lse = lse(column_lse(0, masked), column_lse(1))

    def off_chip(k):
        for half in range(2):
            far_copy(half, k).wait_recv()
        pass_copy(k).start()
        add_scores(2, k)

        @pl.when(k > 0)
        def _():
            pass_copy(k - 1).wait_recv()
            add_scores(3, k - 1)

    loop(off_chip)
    far_lse = column_lse(2)
    pass_copy(chunks - 1).wait_recv()
    add_scores(3, chunks - 1)

    theirs = row_lse(3)
    post(0, as_row(theirs), f)
    local = merged(lse(chip_lse, far_lse, column_lse(3)))
    post(1, local, g)
    message(0, f).wait_recv()
    norm = lse(local, in_msg[0, :1, :])
    post(2, norm, p)
    post(3, norm, r)
    norm_ref[...] = jnp.broadcast_to(norm, (8, rows))
    norm_row = jnp.concatenate([norm, norm], axis=1)
    message(1, g).wait_recv()
    weigh(3, lse(as_column(in_msg[1, :1, :]), theirs), norm_row)

    def product(k):
        value = SCALE * jnp.dot(w[3 * both : 4 * both, :], x[0:both, columns(k)], preferred_element_type=jnp.float32)
        going[:, columns(k)] = value.astype(jnp.bfloat16)
        grad_copy(k).start()

    loop(product)

    stat[...] = jnp.broadcast_to(as_column(norm_row), (both, 128))

    def weigh_own(c, _):
        row, col = own_index(c)
        same = lax.rem(row, rows) == lax.rem(col, rows)
        tile = strip(0, c)
        across = jnp.exp(tile - norm_row)
        value = across + jnp.exp(tile - stat[pl.ds(pl.multiple_of(c * STRIP, STRIP), STRIP), :1])
        on_diagonal = jnp.where((row >= rows) == (col >= rows), 0.0, across - 1.0)
        value = jnp.where(same, on_diagonal, value)
        wt[pl.ds(pl.multiple_of(c * STRIP, STRIP), STRIP), 0:both] = value.astype(jnp.bfloat16)
        return 0

    lax.fori_loop(0, strips, weigh_own, 0)
    message(2, p).wait_recv()
    weigh(1, as_column(in_msg[2, :1, :]), norm_row)
    message(3, r).wait_recv()
    weigh(2, as_column(in_msg[3, :1, :]), norm_row)
    for block in (1, 2, 3):
        turn(block)

    def local_gradient(k):
        value = SCALE * jnp.dot(wt[...], x[:, columns(k)], preferred_element_type=jnp.float32)
        lq_ref[:, columns(k)] = value[:rows]
        ld_ref[:, columns(k)] = value[rows:]

    loop(local_gradient)

    def ends(k):
        for half in range(2):
            near_copy(half, k).wait_send()
            far_copy(half, k).wait_send()
        pass_copy(k).wait_send()
        grad_copy(k).wait_send()
        grad_copy(k).wait_recv()

    for which, to in enumerate((f, g, p, r)):
        message(which, to).wait_send()
    loop(ends)


def on_device(queries, documents, count):
    rows, depth = queries.shape
    both = 2 * rows
    chunks = depth // WIDTH
    dma = pltpu.SemaphoreType.DMA
    norm, part_q, part_d, came = pl.pallas_call(
        functools.partial(kernel, count),
        out_shape=(
            jax.ShapeDtypeStruct((8, rows), jnp.float32),
            pltpu.VMEM((rows, depth), jnp.float32),
            pltpu.VMEM((rows, depth), jnp.float32),
            pltpu.VMEM((both, depth), jnp.bfloat16),
        ),
        in_specs=[pl.BlockSpec(memory_space=pltpu.HBM)] * 2,
        out_specs=(pl.BlockSpec(memory_space=pltpu.VMEM),) * 4,
        scratch_shapes=[
            pltpu.VMEM((4 * both, depth), jnp.bfloat16),
            pltpu.VMEM((4 * both, both), jnp.float32),
            pltpu.VMEM((4 * both, both), jnp.bfloat16),
            pltpu.VMEM((both, 4 * both), jnp.bfloat16),
            pltpu.VMEM((both, depth), jnp.bfloat16),
            pltpu.VMEM((both, 128), jnp.float32),
            pltpu.VMEM((4, 8, rows), jnp.float32),
            pltpu.VMEM((4, 8, rows), jnp.float32),
            dma((2, chunks)),
            dma((2, chunks)),
            dma((2, chunks)),
            dma((2, chunks)),
            dma((2, chunks)),
            dma((chunks,)),
            dma((chunks,)),
            dma((chunks,)),
            dma((chunks,)),
            dma((4,)),
            dma((4,)),
        ],
        compiler_params=pltpu.CompilerParams(
            collective_id=0, has_side_effects=True, vmem_limit_bytes=44 << 20
        ),
    )(queries, documents)
    came = came.astype(jnp.float32)
    return norm[0], part_q + came[:rows], part_d + came[rows:]


def solution(mesh):
    return jax.shard_map(
        functools.partial(on_device, count=mesh.shape["dp"]),
        mesh=mesh,
        in_specs=(P("dp", None), P("dp", None)),
        out_specs=(P("dp"), P("dp", None), P("dp", None)),
        check_vma=False,
    )
```

time: 357 us -> 122 us (0.34)
  waiting for transfers between devices: 275 us -> 0 us
  Pallas kernels: 0 us -> 108 us
  matrix products: 42.6 us -> 0 us
  starting transfers between devices: 35.6 us -> 0 us
  other arithmetic: 1.43 us -> 11.4 us
    ppermute x14 -> x0, waiting for transfers between devices: 275 us -> none  [passed_along(): return lax.ppermute(value, axis, pairs)]
    pallas_call x0 -> x1, Pallas kernels: none -> 108 us  [on_device(): pl.pallas_call(functools.partial(kernel, count), out_shape=(jax.ShapeDtyp...]
    dot_general x31 -> x0, matrix products: 42.6 us -> none  [the longest x9 20.3 us: transposed_product(): lax.dot_general(weights, values, (((0,), (0,)), ((), ())), preferred_elem...]
    ppermute x14 -> x0, starting transfers between devices: 35.6 us -> none  [passed_along(): return lax.ppermute(value, axis, pairs)]
    add x3 -> x1, other arithmetic: 0.03 us -> 7.51 us  [on_device(): return (norm[0], part_q + came[:rows], part_d + came[rows:])]
    convert_element_type x0 -> x1, other arithmetic: none -> 3.92 us  [on_device(): came = came.astype(jnp.float32)]
  transfers between devices with their start and end apart: 14 -> 0, of which waited for: 9 -> 0; matrix products, arithmetic and copies ran while one was open for 11% -> 0% of each run, Pallas kernels for 0% -> 0%
where the time goes in v1:
time: 122 us; the launch traced here: 121 us
  Pallas kernels  108 us (89%)
  other arithmetic  11.4 us (9%)
  local copies, waits for them, and re-layouts  1.26 us (1%)
    pallas_call x1, Pallas kernels, on_device(): pl.pallas_call(functools.partial(kernel, count), out_shape=(jax.ShapeDtyp...  108 us
    add x1, other arithmetic, on_device(): return (norm[0], part_q + came[:rows], part_d + came[rows:])  7.51 us
    convert_element_type x1, other arithmetic, on_device(): came = came.astype(jnp.float32)  3.92 us

profile of v1, /device:TPU:1, one launch (start us, length us, event | category | flops | bytes accessed | tf_op | source)
XLA Modules:
  0.0 121.3 jit_solution(6207618241151372463)
XLA Ops:
  0.6 108.0 %shard_map.49 = (f32[8,256]{1,0:T(8,128)}, f32[256,3584]{1,0:T(8,128)S(1)}, f32[256,3584]{1,0:T(8,128)S(1)}, bf16[512,3584]{1,0:T(8,128)(2,1)S(1)}) custom-call(bf16[256,3584]{1,0:T(8,128)(2,1)} %q_ref.1, bf16[256,3584]{1,0:T(8,128)(2,1)} %d_ref.1), custom_call_target="tpu_custom_call" | custom-call | tf_op jit(solution)/shard_map/pallas_call | solution.py:307
  108.6 1.3 %slice.9 = f32[1,256]{1,0:T(1,128)} slice(f32[8,256]{1,0:T(8,128)} %get-tuple-element.7), slice={[0:1], [0:256]} | slice | bytes 2048 | tf_op jit(solution)/shard_map/slice | solution.py:343
  109.9 3.9 %convert_element_type.3 = f32[512,3584]{1,0:T(8,128)} convert(bf16[512,3584]{1,0:T(8,128)(2,1)S(1)} %get-tuple-element.9) | non-fusion elementwise | flops 1835008 | bytes 11010048 | tf_op jit(solution)/shard_map/convert_element_type | solution.py:342
  113.8 7.5 %slice_add_fusion = (f32[256,3584]{1,0:T(8,128)}, f32[256,3584]{1,0:T(8,128)}) fusion(f32[256,3584]{1,0:T(8,128)S(1)} %get-tuple-element.10, f32[512,3584]{1,0:T(8,128)} %convert_element_type.3, f32[256,3584]{1,0:T(8,128)S(1)} %get-tuple-element.8), kind=kLoop, calls=%fused_computation | loop fusion | flops 1835008 | bytes 22020096 | tf_op jit(solution)/shard_map/add | solution.py:343

commit v2 on v1

v2 whole, which is shorter than its diff:
```python
import functools

import jax
import jax.numpy as jnp
from jax import lax
from jax.experimental import pallas as pl
from jax.experimental.pallas import tpu as pltpu
from jax.sharding import PartitionSpec as P

MESH = pl.DeviceIdType.MESH
SCALE = 100.0
WIDTH = 512
GROUP = 128


def lse(*terms):
    highest = functools.reduce(jnp.maximum, terms)
    return highest + jnp.log(sum(jnp.exp(term - highest) for term in terms))


def as_column(row):
    return jnp.broadcast_to(row, (128, row.shape[1])).T[:, :1]


def as_row(column):
    return jnp.broadcast_to(column, (column.shape[0], 128)).T[:1, :]


def cross(left, right):
    return lax.dot_general(left, right, (((1,), (1,)), ((), ())), preferred_element_type=jnp.float32)


def kernel(
    count,
    q_ref,
    d_ref,
    norm_ref,
    lq_ref,
    ld_ref,
    x,
    s,
    w,
    wt,
    going,
    came,
    stat,
    out_msg,
    in_msg,
    own_sem,
    near_send,
    near_recv,
    far_send,
    far_recv,
    pass_send,
    pass_recv,
    grad_send,
    grad_recv,
    msg_send,
    msg_recv,
):
    rows, depth = q_ref.shape
    both = 2 * rows
    chunks = depth // WIDTH
    groups = both // GROUP
    me = lax.axis_index("dp")
    sign = 1 - 2 * lax.rem(me, 2)
    p = me + sign
    r = lax.rem(me - sign + count, count)
    f = lax.rem(me + 2 * sign + count, count)
    g = lax.rem(me - 2 * sign + count, count)

    def remote(src, dst, send, recv, to):
        return pltpu.make_async_remote_copy(
            src_ref=src, dst_ref=dst, send_sem=send, recv_sem=recv, device_id=(to,), device_id_type=MESH
        )

    def columns(k):
        return pl.ds(pl.multiple_of(k * WIDTH, WIDTH), WIDTH)

    def part(block, group):
        return pl.ds(block * both + group * GROUP, GROUP)

    def source(group):
        half, first = divmod(group * GROUP, rows)
        return (q_ref, d_ref)[half].at[pl.ds(first, GROUP), :]

    def own_copy(half, k):
        ref = (q_ref, d_ref)[half]
        return pltpu.make_async_copy(
            ref.at[:, columns(k)], x.at[pl.ds(half * rows, rows), columns(k)], own_sem.at[half, k]
        )

    def near_copy(half, k):
        ref = (q_ref, d_ref)[half]
        return remote(
            ref.at[:, columns(k)],
            x.at[pl.ds(both + half * rows, rows), columns(k)],
            near_send.at[half, k],
            near_recv.at[half, k],
            p,
        )

    def far_copy(group, k):
        return remote(
            source(group).at[:, columns(k)],
            x.at[part(2, group), columns(k)],
            far_send.at[group, k],
            far_recv.at[group, k],
            r,
        )

    def pass_copy(group, k):
        return remote(
            x.at[part(2, group), columns(k)],
            x.at[part(3, group), columns(k)],
            pass_send.at[group, k],
            pass_recv.at[group, k],
            p,
        )

    def grad_copy(group, k):
        at = (pl.ds(group * GROUP, GROUP), columns(k))
        return remote(going.at[at], came.at[at], grad_send.at[group, k], grad_recv.at[group, k], f)

    def message(which, to):
        return remote(out_msg.at[which], in_msg.at[which], msg_send.at[which], msg_recv.at[which], to)

    def add_scores(at, k):
        s[at, :] += cross(x[at, columns(k)], x[0:both, columns(k)])

    def tile(block, group):
        return SCALE * s[part(block, group), :]

    def same_pair(group):
        row = lax.broadcasted_iota(jnp.int32, (GROUP, both), 0) + group * GROUP
        col = lax.broadcasted_iota(jnp.int32, (GROUP, both), 1)
        return (row == col) | (row == col + rows) | (row + rows == col), col < rows

    def column_lse(value):
        top = jnp.max(value, axis=0, keepdims=True)
        return top + jnp.log(jnp.sum(jnp.exp(value - top), axis=0, keepdims=True))

    def row_lse(value):
        top = jnp.max(value, axis=1, keepdims=True)
        return top + jnp.log(jnp.sum(jnp.exp(value - top), axis=1, keepdims=True))

    def post(which, row, to):
        out_msg[which] = jnp.broadcast_to(row, (8, rows))
        message(which, to).start()

    def weigh(block, group, column, row):
        first = group * GROUP % rows
        value = tile(block, group)
        value = jnp.exp(value - column[first : first + GROUP]) + jnp.exp(value - row)
        w[part(block, group), :] = value.astype(jnp.bfloat16)

    def turn(block):
        at = pl.ds(block * both, both)
        wt[:, at] = w[at, :].T

    def loop(body):
        def step(k, _):
            body(k)
            return 0

        lax.fori_loop(0, chunks, step, 0)

    barrier = pltpu.get_barrier_semaphore()
    for device in (p, r, f, g):
        pl.semaphore_signal(barrier, inc=1, device_id=(device,), device_id_type=MESH)
    s[...] = jnp.zeros_like(s)
    pl.semaphore_wait(barrier, 4)

    def send_first(k):
        far_copy(0, k).start()
        for half in range(2):
            own_copy(half, k).start()
            near_copy(half, k).start()

    loop(send_first)
    for group in range(1, groups):
        loop(lambda k: far_copy(group, k).start())

    def on_chip(k):
        for half in range(2):
            own_copy(half, k).wait()
            near_copy(half, k).wait_recv()
        add_scores(pl.ds(0, 2 * both), k)

    loop(on_chip)
    held = []
    for group in range(groups):
        same, query = same_pair(group)
        keep = query if group * GROUP >= rows else False
        held.append(column_lse(jnp.where(same & ~keep, -jnp.inf, tile(0, group))))
        held.append(column_lse(tile(1, group)))
    chip_lse = lse(*held)

    for group in range(groups):

        def off_chip(k):
            far_copy(group, k).wait_recv()
            pass_copy(group, k).start()
            add_scores(part(2, group), k)

            @pl.when(k > 0)
            def _():
                pass_copy(group, k - 1).wait_recv()
                add_scores(part(3, group), k - 1)

        loop(off_chip)
        chip_lse = lse(chip_lse, column_lse(tile(2, group)))
        pass_copy(group, chunks - 1).wait_recv()
        add_scores(part(3, group), chunks - 1)
        value = tile(3, group)
        stat[pl.ds(group * GROUP, GROUP), :] = jnp.broadcast_to(row_lse(value), (GROUP, 128))
        if group < groups - 1:
            chip_lse = lse(chip_lse, column_lse(value))

    theirs = as_row(lse(stat[0:rows, :], stat[rows:both, :]))
    post(0, theirs, f)
    chip_lse = lse(chip_lse, column_lse(value))
    local = lse(chip_lse[:, :rows], chip_lse[:, rows:])
    post(1, local, g)
    message(0, f).wait_recv()
    norm = lse(local, in_msg[0, :1, :])
    norm_row = jnp.concatenate([norm, norm], axis=1)
    message(1, g).wait_recv()
    far_column = as_column(lse(in_msg[1, :1, :], theirs))

    for group in range(groups):
        weigh(3, group, far_column, norm_row)

        def product(k):
            value = jnp.dot(w[part(3, group), :], x[0:both, columns(k)], preferred_element_type=jnp.float32)
            going[pl.ds(group * GROUP, GROUP), columns(k)] = (SCALE * value).astype(jnp.bfloat16)
            grad_copy(group, k).start()

        loop(product)
        if group == 0:
            post(2, norm, p)
            post(3, norm, r)
            norm_ref[...] = norm

    own_column = as_column(norm)
    for group in range(groups):
        same, query = same_pair(group)
        if group * GROUP >= rows:
            query = ~query
        first = group * GROUP % rows
        value = tile(0, group)
        across = jnp.exp(value - norm_row)
        value = across + jnp.exp(value - own_column[first : first + GROUP])
        value = jnp.where(same, jnp.where(query, 0.0, across - 1.0), value)
        wt[pl.ds(group * GROUP, GROUP), 0:both] = value.astype(jnp.bfloat16)
    for block, which, to in ((1, 2, p), (2, 3, r)):
        message(which, to).wait_recv()
        column = as_column(in_msg[which, :1, :])
        for group in range(groups):
            weigh(block, group, column, norm_row)
    for block in (1, 2, 3):
        turn(block)

    def local_gradient(k):
        value = SCALE * jnp.dot(wt[...], x[:, columns(k)], preferred_element_type=jnp.float32)
        lq_ref[:, columns(k)] = value[:rows]
        ld_ref[:, columns(k)] = value[rows:]

    loop(local_gradient)

    def sent(k):
        for half in range(2):
            near_copy(half, k).wait_send()
        for group in range(groups):
            far_copy(group, k).wait_send()
            pass_copy(group, k).wait_send()

    loop(sent)
    for which, to in enumerate((f, g, p, r)):
        message(which, to).wait_send()
    for group in range(groups):
        half, first = divmod(group * GROUP, rows)
        out = (lq_ref, ld_ref)[half]

        def add_terms(k):
            grad_copy(group, k).wait_recv()
            terms = came[pl.ds(group * GROUP, GROUP), columns(k)]
            out[pl.ds(first, GROUP), columns(k)] += terms.astype(jnp.float32)
            grad_copy(group, k).wait_send()

        loop(add_terms)


def on_device(queries, documents, count):
    rows, depth = queries.shape
    both = 2 * rows
    chunks = depth // WIDTH
    groups = both // GROUP
    dma = pltpu.SemaphoreType.DMA
    norm, grad_q, grad_d = pl.pallas_call(
        functools.partial(kernel, count),
        out_shape=(
            jax.ShapeDtypeStruct((1, rows), jnp.float32),
            pltpu.VMEM((rows, depth), jnp.float32),
            pltpu.VMEM((rows, depth), jnp.float32),
        ),
        in_specs=[pl.BlockSpec(memory_space=pltpu.HBM)] * 2,
        out_specs=(pl.BlockSpec(memory_space=pltpu.VMEM),) * 3,
        scratch_shapes=[
            pltpu.VMEM((4 * both, depth), jnp.bfloat16),
            pltpu.VMEM((4 * both, both), jnp.float32),
            pltpu.VMEM((4 * both, both), jnp.bfloat16),
            pltpu.VMEM((both, 4 * both), jnp.bfloat16),
            pltpu.VMEM((both, depth), jnp.bfloat16),
            pltpu.VMEM((both, depth), jnp.bfloat16),
            pltpu.VMEM((both, 128), jnp.float32),
            pltpu.VMEM((4, 8, rows), jnp.float32),
            pltpu.VMEM((4, 8, rows), jnp.float32),
            dma((2, chunks)),
            dma((2, chunks)),
            dma((2, chunks)),
            dma((groups, chunks)),
            dma((groups, chunks)),
            dma((groups, chunks)),
            dma((groups, chunks)),
            dma((groups, chunks)),
            dma((groups, chunks)),
            dma((4,)),
            dma((4,)),
        ],
        compiler_params=pltpu.CompilerParams(
            collective_id=0, has_side_effects=True, vmem_limit_bytes=56 << 20
        ),
    )(queries, documents)
    return norm.reshape(rows), grad_q, grad_d


def solution(mesh):
    return jax.shard_map(
        functools.partial(on_device, count=mesh.shape["dp"]),
        mesh=mesh,
        in_specs=(P("dp", None), P("dp", None)),
        out_specs=(P("dp"), P("dp", None), P("dp", None)),
        check_vma=False,
    )
```

time: 122 us -> 111 us (0.910)
  other arithmetic: 11.4 us -> 0 us
  Pallas kernels: 108 us -> 105 us
  local copies, waits for them, and re-layouts: 1.26 us -> 4.24 us
    add x1 -> x0, other arithmetic: 7.51 us -> none  [on_device(): return (norm[0], part_q + came[:rows], part_d + came[rows:])]
    unnamed x0 -> x5, local copies, waits for them, and re-layouts: none -> 4.24 us
    convert_element_type x1 -> x0, other arithmetic: 3.92 us -> none  [on_device(): came = came.astype(jnp.float32)]
    pallas_call x1, Pallas kernels: 108 us -> 105 us  [on_device(): pl.pallas_call(functools.partial(kernel, count), out_shape=(jax.ShapeDtyp...]
    slice x1 -> x0, local copies, waits for them, and re-layouts: 1.26 us -> none  [on_device(): return (norm[0], part_q + came[:rows], part_d + came[rows:])]
where the time goes in v2:
time: 111 us; the launch traced here: 110 us
  Pallas kernels  105 us (95%)
  local copies, waits for them, and re-layouts  4.24 us (4%)
    pallas_call x1, Pallas kernels, on_device(): pl.pallas_call(functools.partial(kernel, count), out_shape=(jax.ShapeDtyp...  105 us
    unnamed x5, local copies, waits for them, and re-layouts  4.24 us

profile of v2, /device:TPU:1, one launch (start us, length us, event | category | flops | bytes accessed | tf_op | source)
XLA Modules:
  0.0 109.8 jit_solution(17018184788845455130)
XLA Ops:
  0.6 104.9 %shard_map.49 = (f32[1,256]{1,0:T(1,128)}, f32[256,3584]{1,0:T(8,128)S(1)}, f32[256,3584]{1,0:T(8,128)S(1)}) custom-call(bf16[256,3584]{1,0:T(8,128)(2,1)} %q_ref.1, bf16[256,3584]{1,0:T(8,128)(2,1)} %d_ref.1), custom_call_target="tpu_custom_call" | custom-call | tf_op jit(solution)/shard_map/pallas_call | solution.py:300
  105.6 1.8 %copy.8 = f32[256,3584]{1,0:T(8,128)} copy(f32[256,3584]{1,0:T(8,128)S(1)} %get-tuple-element.10) | data formatting | bytes 7340032
  107.4 0.0 copy-start
  107.4 1.8 %copy.9 = f32[256,3584]{1,0:T(8,128)} copy(f32[256,3584]{1,0:T(8,128)S(1)} %get-tuple-element.11) | data formatting | bytes 7340032
  109.2 0.0 copy-done
  109.2 0.6 copy.10
Async XLA Ops:
  107.4 1.8 %copy-start = (f32[1,256]{1,0:T(1,128)S(1)}, f32[1,256]{1,0:T(1,128)}, u32[]{:S(2)}) copy-start(f32[1,256]{1,0:T(1,128)} %get-tuple-element.6) | copy-start | bytes 3076

commit v3 on v2

--- a/solution.py
+++ b/solution.py
@@ -11,6 +11,7 @@
 SCALE = 100.0
 WIDTH = 512
 GROUP = 128
+PIECES = 4
 
 
 def lse(*terms):
@@ -118,6 +119,15 @@
             p,
         )
 
+    def direct_copy():
+        return remote(
+            source(groups - 1).at[:, columns(chunks - 1)],
+            x.at[part(3, groups - 1), columns(chunks - 1)],
+            pass_send.at[groups - 1, chunks - 1],
+            pass_recv.at[groups - 1, chunks - 1],
+            g,
+        )
+
     def grad_copy(group, k):
         at = (pl.ds(group * GROUP, GROUP), columns(k))
         return remote(going.at[at], came.at[at], grad_send.at[group, k], grad_recv.at[group, k], f)
@@ -158,12 +168,12 @@
         at = pl.ds(block * both, both)
         wt[:, at] = w[at, :].T
 
-    def loop(body):
+    def loop(body, steps=chunks):
         def step(k, _):
             body(k)
             return 0
 
-        lax.fori_loop(0, chunks, step, 0)
+        lax.fori_loop(0, steps, step, 0)
 
     barrier = pltpu.get_barrier_semaphore()
     for device in (p, r, f, g):
@@ -178,8 +188,11 @@
             near_copy(half, k).start()
 
     loop(send_first)
-    for group in range(1, groups):
+    for group in range(1, groups - 1):
         loop(lambda k: far_copy(group, k).start())
+    loop(lambda k: far_copy(groups - 1, k).start(), chunks - 1)
+    direct_copy().start()
+    far_copy(groups - 1, chunks - 1).start()
 
     def on_chip(k):
         for half in range(2):
@@ -208,18 +221,28 @@
                 pass_copy(group, k - 1).wait_recv()
                 add_scores(part(3, group), k - 1)
 
-        loop(off_chip)
-        chip_lse = lse(chip_lse, column_lse(tile(2, group)))
+        last = group == groups - 1
+        loop(off_chip, chunks - 1)
+        if not last:
+            far_copy(group, chunks - 1).wait_recv()
+            pass_copy(group, chunks - 1).start()
+            add_scores(part(2, group), chunks - 1)
+        pass_copy(group, chunks - 2).wait_recv()
+        add_scores(part(3, group), chunks - 2)
         pass_copy(group, chunks - 1).wait_recv()
         add_scores(part(3, group), chunks - 1)
         value = tile(3, group)
         stat[pl.ds(group * GROUP, GROUP), :] = jnp.broadcast_to(row_lse(value), (GROUP, 128))
-        if group < groups - 1:
+        if last:
+            theirs = as_row(lse(stat[0:rows, :], stat[rows:both, :]))
+            post(0, theirs, f)
             chip_lse = lse(chip_lse, column_lse(value))
-
-    theirs = as_row(lse(stat[0:rows, :], stat[rows:both, :]))
-    post(0, theirs, f)
-    chip_lse = lse(chip_lse, column_lse(value))
+            far_copy(group, chunks - 1).wait_recv()
+            add_scores(part(2, group), chunks - 1)
+            chip_lse = lse(chip_lse, column_lse(tile(2, group)))
+        else:
+            chip_lse = lse(chip_lse, column_lse(value), column_lse(tile(2, group)))
+
     local = lse(chip_lse[:, :rows], chip_lse[:, rows:])
     post(1, local, g)
     message(0, f).wait_recv()
@@ -273,9 +296,15 @@
             near_copy(half, k).wait_send()
         for group in range(groups):
             far_copy(group, k).wait_send()
+
+    def passed(k):
+        for group in range(groups - 1):
             pass_copy(group, k).wait_send()
 
     loop(sent)
+    loop(passed)
+    loop(lambda k: pass_copy(groups - 1, k).wait_send(), chunks - 1)
+    direct_copy().wait_send()
     for which, to in enumerate((f, g, p, r)):
         message(which, to).wait_send()
     for group in range(groups):
@@ -289,6 +318,20 @@
             grad_copy(group, k).wait_send()
 
         loop(add_terms)
+
+
+def write_out(norm_in, q_in, d_in, norm_out, q_out, d_out, sem):
+    copies = []
+    rows = q_in.shape[0] // PIECES
+    for which, (source, target) in enumerate(((q_in, q_out), (d_in, d_out))):
+        for piece in range(PIECES):
+            at = pl.ds(piece * rows, rows)
+            copies.append(pltpu.make_async_copy(source.at[at, :], target.at[at, :], sem.at[which, piece]))
+    copies.append(pltpu.make_async_copy(norm_in, norm_out, sem.at[2, 0]))
+    for copy in copies:
+        copy.start()
+    for copy in copies:
+        copy.wait()
 
 
 def on_device(queries, documents, count):
@@ -300,7 +343,7 @@
     norm, grad_q, grad_d = pl.pallas_call(
         functools.partial(kernel, count),
         out_shape=(
-            jax.ShapeDtypeStruct((1, rows), jnp.float32),
+            pltpu.VMEM((1, rows), jnp.float32),
             pltpu.VMEM((rows, depth), jnp.float32),
             pltpu.VMEM((rows, depth), jnp.float32),
         ),
@@ -332,6 +375,18 @@
             collective_id=0, has_side_effects=True, vmem_limit_bytes=56 << 20
         ),
     )(queries, documents)
+    norm, grad_q, grad_d = pl.pallas_call(
+        write_out,
+        out_shape=(
+            jax.ShapeDtypeStruct((1, rows), jnp.float32),
+            jax.ShapeDtypeStruct((rows, depth), jnp.float32),
+            jax.ShapeDtypeStruct((rows, depth), jnp.float32),
+        ),
+        in_specs=[pl.BlockSpec(memory_space=pltpu.VMEM)] * 3,
+        out_specs=(pl.BlockSpec(memory_space=pl.ANY),) * 3,
+        scratch_shapes=[dma((3, PIECES))],
+        compiler_params=pltpu.CompilerParams(vmem_limit_bytes=16 << 20),
+    )(*[pltpu.with_memory_space_constraint(a, pltpu.VMEM) for a in (norm, grad_q, grad_d)])
     return norm.reshape(rows), grad_q, grad_d
 
 

time: 111 us -> 109 us (0.982)
  local copies, waits for them, and re-layouts: 4.24 us -> 0 us
  Pallas kernels: 105 us -> 108 us
    unnamed x5 -> x0, local copies, waits for them, and re-layouts: 4.24 us -> none
    pallas_call x1 -> x2, Pallas kernels: 105 us -> 108 us  [the longest x1 105 us: on_device(): pl.pallas_call(functools.partial(kernel, count), out_shape=(pltpu.VMEM((1...]
where the time goes in v3:
time: 109 us
  Pallas kernels  108 us (99%)
    pallas_call x1, Pallas kernels, on_device(): pl.pallas_call(functools.partial(kernel, count), out_shape=(pltpu.VMEM((1...  105 us
    pallas_call x1, Pallas kernels, on_device(): pl.pallas_call(write_out, out_shape=(jax.ShapeDtypeStruct((1, rows), jnp....  3.09 us

profile of v3, /device:TPU:1, one launch (start us, length us, event | category | flops | bytes accessed | tf_op | source)
XLA Modules:
  0.0 108.6 jit_solution(13797007976006427795)
XLA Ops:
  0.6 104.9 %shard_map.49 = (f32[1,256]{1,0:T(1,128)S(1)}, f32[256,3584]{1,0:T(8,128)S(1)}, f32[256,3584]{1,0:T(8,128)S(1)}) custom-call(bf16[256,3584]{1,0:T(8,128)(2,1)} %q_ref.1, bf16[256,3584]{1,0:T(8,128)(2,1)} %d_ref.1), custom_call_target="tpu_custom_call" | custom-call | tf_op jit(solution)/shard_map/pallas_call | solution.py:343
  105.5 3.1 %shard_map.50 = (f32[1,256]{1,0:T(1,128)}, f32[256,3584]{1,0:T(8,128)}, f32[256,3584]{1,0:T(8,128)}) custom-call(f32[1,256]{1,0:T(1,128)S(1)} %get-tuple-element.9.norm_in, f32[256,3584]{1,0:T(8,128)S(1)} %get-tuple-element.10.q_in, f32[256,3584]{1,0:T(8,128)S(1)} %get-tuple-element.11.d_in), custom_call_target="tpu_custom_call" | custom-call | tf_op jit(solution)/shard_map/pallas_call | solution.py:378

commit v4 on v3

--- a/solution.py
+++ b/solution.py
@@ -11,7 +11,7 @@
 SCALE = 100.0
 WIDTH = 512
 GROUP = 128
-PIECES = 4
+PIECES = 8
 
 
 def lse(*terms):
@@ -158,10 +158,8 @@
         out_msg[which] = jnp.broadcast_to(row, (8, rows))
         message(which, to).start()
 
-    def weigh(block, group, column, row):
-        first = group * GROUP % rows
-        value = tile(block, group)
-        value = jnp.exp(value - column[first : first + GROUP]) + jnp.exp(value - row)
+    def weigh(block, group, column, across):
+        value = across + jnp.exp(tile(block, group) - column)
         w[part(block, group), :] = value.astype(jnp.bfloat16)
 
     def turn(block):
@@ -248,11 +246,18 @@
     message(0, f).wait_recv()
     norm = lse(local, in_msg[0, :1, :])
     norm_row = jnp.concatenate([norm, norm], axis=1)
+
+    def across(block, group):
+        return jnp.exp(tile(block, group) - norm_row)
+
+    early = across(3, 0)
     message(1, g).wait_recv()
-    far_column = as_column(lse(in_msg[1, :1, :], theirs))
+    far_norm = lse(in_msg[1, :1, :], theirs)
 
     for group in range(groups):
-        weigh(3, group, far_column, norm_row)
+        first = group * GROUP % rows
+        column = as_column(far_norm[:, first : first + GROUP])
+        weigh(3, group, column, across(3, group) if group else early)
 
         def product(k):
             value = jnp.dot(w[part(3, group), :], x[0:both, columns(k)], preferred_element_type=jnp.float32)
@@ -272,15 +277,16 @@
             query = ~query
         first = group * GROUP % rows
         value = tile(0, group)
-        across = jnp.exp(value - norm_row)
-        value = across + jnp.exp(value - own_column[first : first + GROUP])
-        value = jnp.where(same, jnp.where(query, 0.0, across - 1.0), value)
+        one = across(0, group)
+        value = one + jnp.exp(value - own_column[first : first + GROUP])
+        value = jnp.where(same, jnp.where(query, 0.0, one - 1.0), value)
         wt[pl.ds(group * GROUP, GROUP), 0:both] = value.astype(jnp.bfloat16)
     for block, which, to in ((1, 2, p), (2, 3, r)):
         message(which, to).wait_recv()
         column = as_column(in_msg[which, :1, :])
         for group in range(groups):
-            weigh(block, group, column, norm_row)
+            first = group * GROUP % rows
+            weigh(block, group, column[first : first + GROUP], across(block, group))
     for block in (1, 2, 3):
         turn(block)
 

time: 109 us -> 109 us (level)
  no operation moved by 1% of the time
where the time goes in v4:
time: 109 us
  Pallas kernels  108 us (99%)
    pallas_call x1, Pallas kernels, on_device(): pl.pallas_call(functools.partial(kernel, count), out_shape=(pltpu.VMEM((1...  105 us
    pallas_call x1, Pallas kernels, on_device(): pl.pallas_call(write_out, out_shape=(jax.ShapeDtypeStruct((1, rows), jnp....  3.18 us

profile of v4, /device:TPU:1, one launch (start us, length us, event | category | flops | bytes accessed | tf_op | source)
XLA Modules:
  0.0 108.7 jit_solution(8851441635488079084)
XLA Ops:
  0.6 104.9 %shard_map.49 = (f32[1,256]{1,0:T(1,128)S(1)}, f32[256,3584]{1,0:T(8,128)S(1)}, f32[256,3584]{1,0:T(8,128)S(1)}) custom-call(bf16[256,3584]{1,0:T(8,128)(2,1)} %q_ref.1, bf16[256,3584]{1,0:T(8,128)(2,1)} %d_ref.1), custom_call_target="tpu_custom_call" | custom-call | tf_op jit(solution)/shard_map/pallas_call | solution.py:349
  105.5 3.2 %shard_map.50 = (f32[1,256]{1,0:T(1,128)}, f32[256,3584]{1,0:T(8,128)}, f32[256,3584]{1,0:T(8,128)}) custom-call(f32[1,256]{1,0:T(1,128)S(1)} %get-tuple-element.9.norm_in, f32[256,3584]{1,0:T(8,128)S(1)} %get-tuple-element.10.q_in, f32[256,3584]{1,0:T(8,128)S(1)} %get-tuple-element.11.d_in), custom_call_target="tpu_custom_call" | custom-call | tf_op jit(solution)/shard_map/pallas_call | solution.py:384

commit v5 on v3

--- a/solution.py
+++ b/solution.py
@@ -178,21 +178,24 @@
     barrier = pltpu.get_barrier_semaphore()
     for device in (p, r, f, g):
         pl.semaphore_signal(barrier, inc=1, device_id=(device,), device_id_type=MESH)
-    s[...] = jnp.zeros_like(s)
-    pl.semaphore_wait(barrier, 4)
-
-    def send_first(k):
-        far_copy(0, k).start()
+
+    def read_own(k):
         for half in range(2):
             own_copy(half, k).start()
+
+    def send_near(k):
+        for half in range(2):
             near_copy(half, k).start()
 
-    loop(send_first)
-    for group in range(1, groups - 1):
+    loop(read_own)
+    pl.semaphore_wait(barrier, 4)
+    for group in range(groups - 1):
         loop(lambda k: far_copy(group, k).start())
     loop(lambda k: far_copy(groups - 1, k).start(), chunks - 1)
     direct_copy().start()
     far_copy(groups - 1, chunks - 1).start()
+    loop(send_near)
+    s[...] = jnp.zeros_like(s)
 
     def on_chip(k):
         for half in range(2):

time: 109 us -> 109 us (level)
  no operation moved by 1% of the time
where the time goes in v5:
time: 109 us
  Pallas kernels  108 us (99%)
    pallas_call x1, Pallas kernels, on_device(): pl.pallas_call(functools.partial(kernel, count), out_shape=(pltpu.VMEM((1...  105 us
    pallas_call x1, Pallas kernels, on_device(): pl.pallas_call(write_out, out_shape=(jax.ShapeDtypeStruct((1, rows), jnp....  3.09 us

profile of v5, /device:TPU:1, one launch (start us, length us, event | category | flops | bytes accessed | tf_op | source)
XLA Modules:
  0.0 108.6 jit_solution(5493616205030111073)
XLA Ops:
  0.6 104.9 %shard_map.49 = (f32[1,256]{1,0:T(1,128)S(1)}, f32[256,3584]{1,0:T(8,128)S(1)}, f32[256,3584]{1,0:T(8,128)S(1)}) custom-call(bf16[256,3584]{1,0:T(8,128)(2,1)} %q_ref.1, bf16[256,3584]{1,0:T(8,128)(2,1)} %d_ref.1), custom_call_target="tpu_custom_call" | custom-call | tf_op jit(solution)/shard_map/pallas_call | solution.py:346
  105.5 3.1 %shard_map.50 = (f32[1,256]{1,0:T(1,128)}, f32[256,3584]{1,0:T(8,128)}, f32[256,3584]{1,0:T(8,128)}) custom-call(f32[1,256]{1,0:T(1,128)S(1)} %get-tuple-element.9.norm_in, f32[256,3584]{1,0:T(8,128)S(1)} %get-tuple-element.10.q_in, f32[256,3584]{1,0:T(8,128)S(1)} %get-tuple-element.11.d_in), custom_call_target="tpu_custom_call" | custom-call | tf_op jit(solution)/shard_map/pallas_call | solution.py:381
